TPU v7x, 32 devices: a whole 2x2x4 slice. The times are simulated.
32 devices in a mesh: groups: 2 (over y), tensor: 4 (over z), req: 2 (over x), pair: 2 (over core).
Axes of the slice: x: 2, y: 2, z: 4, core: 2. Of those that a mesh axis runs over, the one named last changes fastest.
Arguments:
- residual_input: bfloat16 [4, 64, 8192], P(('groups', 'pair'), None, ('req', 'tensor')), parts along dimension 0
- contexts: bfloat16 [2, 4, 64, 8192], P(None, ('groups', 'pair'), 'req', 'tensor'), parts along dimension 1, may hold values from -6 to 6
- projection_weight: bfloat16 [2, 8192, 8192], P(None, 'tensor', 'req'), may hold values from -0.0625 to 0.0625
- adapter_down_factors: bfloat16 [2, 64, 8192, 64], P(None, ('req', 'pair'), 'tensor'), may hold values from -0.0625 to 0.0625
- adapter_up_factors: bfloat16 [2, 64, 64, 8192], P(None, None, None, ('req', 'tensor')), may hold values from -0.75 to 0.75
- norm_gain_vector: bfloat16 [8192], P(('req', 'tensor')), may hold values from 0.5 to 1.5
- request_adapter_index: int32 [4, 64], P('groups'), parts along dimension 0, may hold values from 0 to 63, as said below
Outputs:
- residual_out: bfloat16 [4, 64, 8192], P(('groups', 'pair'), None, ('req', 'tensor')), parts along dimension 0
- normed: bfloat16 [4, 64, 8192], P(('groups', 'pair'), None, ('req', 'tensor')), parts along dimension 0
There are 2 independent parts, one for each index of `groups`. A program takes and returns all parts, laid end to end along the dimension named above; an argument that names none is the same for every part. Nothing has to cross between parts.
Inputs may be any that keep to these rules, and one draw needn't show every extreme that they name: `request_adapter_index`: owner o holds adapters o * 16 to (o + 1) * 16 - 1. The requests r * 32 to (r + 1) * 32 - 1 of one half use exactly 4 different adapters, at most 2 of them held by one owner, and exactly 2 by some owner.
All inputs are finite; a program needn't handle non-finite values.
Results may differ from a plain program's by a relative error of at most 0.0085.
Values may be sent and summed in bfloat16 or wider, within the bound.
A program may use at most 256 MiB of HBM per device.

v0:
```python
import jax
import jax.numpy as jnp
from jax import lax
from jax.sharding import PartitionSpec as P

MODEL_WIDTH = 8192
DECODER_LAYERS = 2


adapter_scale = 2.0
norm_eps = 1e-05


def shards(
    residual_input,
    contexts,
    projection_weight,
    adapter_down_factors,
    adapter_up_factors,
    norm_gain_vector,
    request_adapter_index,
):
    req_count = contexts.shape[2]
    half_index = lax.axis_index("pair")
    req_index = lax.axis_index("req")
    index_half_split = lax.dynamic_index_in_dim(
        request_adapter_index, half_index, 0, keepdims=False
    )
    ids_own = lax.dynamic_slice_in_dim(index_half_split, req_index * req_count, req_count, 0)
    hidden_state = residual_input[0]
    for layer_number in range(DECODER_LAYERS):
        context_own = contexts[layer_number, 0]
        context_all = lax.all_gather(context_own, "req", axis=0, tiled=True)
        weight_layer = projection_weight[layer_number]
        base_product = lax.psum_scatter(
            lax.dot_general(
                weight_layer,
                context_all,
                (((0,), (1,)), ((), ())),
                preferred_element_type=jnp.float32,
            ),
            "tensor",
            scatter_dimension=0,
            tiled=True,
        ).T
        layer_down_factor = adapter_down_factors[layer_number]
        whole_pool = lax.all_gather(layer_down_factor, ("req", "pair"), axis=0, tiled=True)
        blocks = whole_pool[ids_own]
        partial_value = jnp.einsum(
            "ik,ikr->ir", context_own, blocks, preferred_element_type=jnp.float32
        )
        shrink_own = lax.psum(partial_value, "tensor").astype(jnp.bfloat16)
        shrink_all = lax.all_gather(shrink_own, "req", axis=0, tiled=True)
        selected_up_factor = adapter_up_factors[layer_number][index_half_split]
        expand_product = jnp.einsum(
            "ir,irc->ic", shrink_all, selected_up_factor, preferred_element_type=jnp.float32
        )
        hidden_state = (
            hidden_state.astype(jnp.float32) + base_product + adapter_scale * expand_product
        ).astype(jnp.bfloat16)
    wide = hidden_state.astype(jnp.float32)
    squares = lax.psum(jnp.sum(wide * wide, axis=-1), ("tensor", "req"))
    mean_square = squares / MODEL_WIDTH
    normed = (
        wide
        * lax.rsqrt(mean_square + norm_eps)[:, None]
        * norm_gain_vector.astype(jnp.float32)[None, :]
    )
    return (hidden_state[None], normed.astype(jnp.bfloat16)[None])


def solution(mesh):
    in_specs = (
        P(("groups", "pair"), None, ("req", "tensor")),
        P(None, ("groups", "pair"), "req", "tensor"),
        P(None, "tensor", "req"),
        P(None, ("req", "pair"), "tensor", None),
        P(None, None, None, ("req", "tensor")),
        P(("req", "tensor")),
        P("groups", None),
    )
    out_specs = (
        P(("groups", "pair"), None, ("req", "tensor")),
        P(("groups", "pair"), None, ("req", "tensor")),
    )
    return jax.shard_map(shards, mesh=mesh, in_specs=in_specs, out_specs=out_specs, check_vma=False)
```

profile of v0, /device:TPU:0, one launch (start us, length us, event | category | flops | bytes accessed | tf_op | source)
XLA Modules:
  0.0 316.3 jit_solution(13934751846376027930)
XLA Ops:
  8.0 0.0 all-gather.7.cloned.1.call-start
  8.0 6.0 %slice_bitcast_fusion.3 = (bf16[1,16,2048,64]{2,3,0,1:T(8,128)(2,1)}, bf16[1,16,2048,64]{2,3,0,1:T(8,128)(2,1)}) fusion(bf16[2,16,2048,64]{2,3,1,0:T(8,128)(2,1)} %param.10), kind=kLoop, calls=%fused_computation.13 | loop fusion | bytes 16777216
  14.1 0.0 copy-start.2
  14.1 0.0 all-gather.7.cloned.1.call-update
  14.1 0.0 all-gather.9.cloned.1.call-start
  14.1 0.7 all-gather.9.cloned.1.call-update
  14.8 0.0 reduce-scatter.3.cloned.1.call-start
  14.9 0.1 copy-done.2
  15.1 7.1 %all-gather = bf16[1,1,64,2048]{3,2,1,0:T(8,128)(2,1)S(1)} all-gather(bf16[1,1,32,2048]{3,2,1,0:T(8,128)(2,1)S(1)} %get-tuple-element.10), channel_id=2, replica_groups=mesh['groups'=2,'tensor'=4,'req'=2,'pair'=2] {'req'}, dimensions={2}, use_global_device_ids=true | all-gather | bytes 393216 | tf_op jit(solution)/shard_map/all_gather | solution.py:33
  22.1 11.1 %fusion.2 = f32[4096,64]{0,1:T(8,128)} fusion(bf16[2,2048,4096]{2,1,0:T(8,128)(2,1)} %param.9, bf16[1,1,64,2048]{3,2,1,0:T(8,128)(2,1)S(1)} %all-gather), kind=kOutput, calls=%fused_computation.6 | convolution fusion | flops 1073741824 | bytes 18087936 | tf_op jit(solution)/shard_map/dot_general | solution.py:36
  33.2 0.0 reduce-scatter.3.cloned.1.call-update
  33.3 0.0 reduce-scatter.5.cloned.1.call-start
  33.3 9.1 %all-gather.2 = bf16[1,1,64,2048]{3,2,1,0:T(8,128)(2,1)S(1)} all-gather(bf16[1,1,32,2048]{3,2,1,0:T(8,128)(2,1)S(1)} %get-tuple-element.13), channel_id=4, replica_groups=mesh['groups'=2,'tensor'=4,'req'=2,'pair'=2] {'req'}, dimensions={2}, use_global_device_ids=true | all-gather | bytes 393216 | tf_op jit(solution)/shard_map/all_gather | solution.py:33
  42.4 0.0 copy-start.5
  42.4 8.6 %fusion = f32[4096,64]{0,1:T(8,128)} fusion(bf16[2,2048,4096]{2,1,0:T(8,128)(2,1)} %param.9, bf16[1,1,64,2048]{3,2,1,0:T(8,128)(2,1)S(1)} %all-gather.2), kind=kOutput, calls=%fused_computation.4 | convolution fusion | flops 1073741824 | bytes 18087936 | tf_op jit(solution)/shard_map/dot_general | solution.py:36
  51.0 0.0 reduce-scatter.5.cloned.1.call-update
  51.0 0.0 copy-done.5
  51.0 0.1 fusion.24
  51.1 12.3 %slice_bitcast_fusion.1 = (bf16[64,64,1024]{2,1,0:T(8,128)(2,1)}, bf16[64,64,1024]{2,1,0:T(8,128)(2,1)}) fusion(bf16[2,64,64,1024]{3,2,1,0:T(8,128)(2,1)} %param.11), kind=kLoop, calls=%fused_computation.11 | loop fusion | bytes 33554432 | tf_op jit(solution)/shard_map/squeeze | solution.py:54
  63.4 8.9 %gather_fusion.1 = bf16[64,64,1024]{2,1,0:T(8,128)(2,1)} fusion(bf16[64,64,1024]{2,1,0:T(8,128)(2,1)} %get-tuple-element.6, s32[1024]{0:T(1024)S(1)} %pad_clamp_fusion), kind=kCustom, calls=%fused_computation.1 | custom fusion | bytes 16777472 | tf_op jit(solution)/shard_map/gather | solution.py:54
  72.3 0.0 copy-start.4
  72.3 9.0 %gather_fusion.3 = bf16[64,64,1024]{2,1,0:T(8,128)(2,1)} fusion(bf16[64,64,1024]{2,1,0:T(8,128)(2,1)} %get-tuple-element.7, s32[1024]{0:T(1024)S(1)} %pad_clamp_fusion), kind=kCustom, calls=%fused_computation.3 | custom fusion | bytes 16777472 | tf_op jit(solution)/shard_map/gather | solution.py:54
  81.3 0.0 copy-done.4
  81.3 44.3 %all-gather.7.cloned.1.call-done = bf16[1,64,2048,64]{2,3,0,1:T(8,128)(2,1)} async-done(((bf16[1,16,2048,64]{2,3,0,1:T(8,128)(2,1)}), bf16[1,64,2048,64]{2,3,0,1:T(8,128)(2,1)}) %all-gather.7.cloned.1.call-update) | async-done | bytes 16777232 | tf_op jit(solution)/shard_map/all_gather | solution.py:47
  125.7 11.6 %gather_fusion = bf16[32,2048,64]{1,2,0:T(8,128)(2,1)} fusion(bf16[64,2048,64]{1,2,0:T(8,128)(2,1)} %bitcast.79, s32[1024]{0:T(1024)S(1)} %pad_clamp_fusion.1), kind=kCustom, calls=%fused_computation | custom fusion | bytes 16777344 | tf_op jit(solution)/shard_map/gather | solution.py:48
  137.3 95.9 %all-gather.9.cloned.1.call-done = bf16[1,64,2048,64]{2,3,0,1:T(8,128)(2,1)} async-done(((bf16[1,16,2048,64]{2,3,0,1:T(8,128)(2,1)}), bf16[1,64,2048,64]{2,3,0,1:T(8,128)(2,1)}) %all-gather.9.cloned.1.call-update) | async-done | bytes 16777232 | tf_op jit(solution)/shard_map/all_gather | solution.py:47
  233.2 10.7 %gather_fusion.2 = bf16[32,2048,64]{1,2,0:T(8,128)(2,1)} fusion(bf16[64,2048,64]{1,2,0:T(8,128)(2,1)} %bitcast.80, s32[1024]{0:T(1024)S(1)} %pad_clamp_fusion.1), kind=kCustom, calls=%fused_computation.2 | custom fusion | bytes 16777344 | tf_op jit(solution)/shard_map/gather | solution.py:48
  243.9 0.0 copy-start
  243.9 5.8 %fusion.17 = f32[32,1,64]{2,1,0:T(1,128)S(1)} fusion(bf16[32,2048,64]{1,2,0:T(8,128)(2,1)} %gather_fusion, bf16[32,2048,1]{1,0,2:T(8,128)(2,1)S(1)} %get-tuple-element.11), kind=kOutput, calls=%fused_computation.31 | convolution fusion | flops 8388608 | bytes 8527872 | tf_op jit(solution)/shard_map/ik,ikr->ir/dot_general | solution.py:49
  249.7 0.0 copy-done
  249.7 2.3 fusion.15
  252.0 19.0 %all-reduce = (bf16[32,64]{1,0:T(8,128)(2,1)S(1)}, bf16[32,64]{1,0:T(8,128)(2,1)S(1)}) all-reduce(f32[32,64]{1,0:T(8,128)S(1)} %bitcast.85, f32[32,64]{1,0:T(8,128)S(1)} %bitcast.84), channel_id=1, replica_groups=mesh['groups'=2,'tensor'=4,'req'=2,'pair'=2] {'tensor'}, use_global_device_ids=true, to_apply=%region_3.4 | all-reduce | flops 4096 | bytes 24576 | tf_op jit(solution)/shard_map/psum | solution.py:52
  271.0 4.4 %all_gather.20 = bf16[64,64]{1,0:T(8,128)(2,1)S(1)} all-gather(bf16[32,64]{1,0:T(8,128)(2,1)S(1)} %get-tuple-element.3), channel_id=1, replica_groups=mesh['groups'=2,'tensor'=4,'req'=2,'pair'=2] {'req'}, dimensions={0}, use_global_device_ids=true | all-gather | bytes 12288 | tf_op jit(solution)/shard_map/all_gather | solution.py:53
  275.3 4.5 %all_gather.23 = bf16[64,64]{1,0:T(8,128)(2,1)S(1)} all-gather(bf16[32,64]{1,0:T(8,128)(2,1)S(1)} %get-tuple-element.2), channel_id=1, replica_groups=mesh['groups'=2,'tensor'=4,'req'=2,'pair'=2] {'req'}, dimensions={0}, use_global_device_ids=true | all-gather | bytes 12288 | tf_op jit(solution)/shard_map/all_gather | solution.py:53
  279.9 4.6 %fusion.22 = f32[64,1,1024]{2,1,0:T(1,128)S(1)} fusion(bf16[64,64,1024]{2,1,0:T(8,128)(2,1)} %gather_fusion.1, bf16[64,64,1]{1,0,2:T(8,128)(2,1)S(1)} %bitcast.82), kind=kOutput, calls=%fused_computation.36 | convolution fusion | flops 8388608 | bytes 8658944 | tf_op jit(solution)/shard_map/ir,irc->ic/dot_general | solution.py:55
  284.5 0.0 copy-start.3
  284.5 4.6 %fusion.20 = f32[64,1,1024]{2,1,0:T(1,128)S(1)} fusion(bf16[64,64,1024]{2,1,0:T(8,128)(2,1)} %gather_fusion.3, bf16[64,64,1]{1,0,2:T(8,128)(2,1)S(1)} %bitcast.83), kind=kOutput, calls=%fused_computation.34 | convolution fusion | flops 8388608 | bytes 8658944 | tf_op jit(solution)/shard_map/ir,irc->ic/dot_general | solution.py:55
  289.1 0.0 reduce-scatter.3.cloned.1.call-done
  289.1 0.0 reduce-scatter.5.cloned.1.call-done
  289.1 0.0 copy-done.3
  289.1 1.3 fusion.6
  290.4 0.0 copy-start.1
  290.4 17.7 %psum.23 = f32[64]{0:T(128)S(1)} all-reduce(f32[64]{0:T(128)S(1)} %get-tuple-element.4), channel_id=1, replica_groups=mesh['groups'=2,'tensor'=4,'req'=2,'pair'=2] {'tensor','req'}, use_global_device_ids=true, to_apply=%region_5.6 | all-reduce | flops 64 | bytes 512 | tf_op jit(solution)/shard_map/psum | solution.py:62
  308.1 0.8 fusion.19
  308.9 0.0 copy-done.1
  (6 shorter events, 0.1 us)
Async XLA Ops:
  8.0 117.7 %all-gather.7.cloned.1.call-start = ((), (), s32[]{:S(2)}) async-start(), calls=%async_computation.4 | async-start | bytes 20971520 | tf_op jit(solution)/shard_map/all_gather | solution.py:47
  14.1 0.9 copy-start.2
  14.1 219.1 %all-gather.9.cloned.1.call-start = ((), (), s32[]{:S(2)}) async-start(), calls=%async_computation.5 | async-start | bytes 20971520 | tf_op jit(solution)/shard_map/all_gather | solution.py:47
  14.8 274.3 %reduce-scatter.3.cloned.1.call-start = ((), (), s32[]{:S(2)}) async-start(), calls=%async_computation.2 | async-start | bytes 1310720 | tf_op jit(solution)/shard_map/reduce_scatter | solution.py:35
  33.3 255.9 %reduce-scatter.5.cloned.1.call-start = ((), (), s32[]{:S(2)}) async-start(), calls=%async_computation.3 | async-start | bytes 1310720 | tf_op jit(solution)/shard_map/reduce_scatter | solution.py:35
  42.4 8.6 %copy-start.5 = (s32[2,64]{1,0:T(2,128)S(1)}, s32[2,64]{1,0:T(2,128)}, u32[]{:S(2)}) copy-start(s32[2,64]{1,0:T(2,128)} %param.13) | copy-start | bytes 1540
  72.3 9.0 %copy-start.4 = (bf16[1024]{0:T(1024)(128)(2,1)S(1)}, bf16[1024]{0:T(1024)(128)(2,1)}, u32[]{:S(2)}) copy-start(bf16[1024]{0:T(1024)(128)(2,1)} %param.12) | copy-start | bytes 6148
  243.9 5.8 %copy-start = (bf16[32,2048,64]{1,2,0:T(8,128)(2,1)S(1)}, bf16[32,2048,64]{1,2,0:T(8,128)(2,1)}, u32[]{:S(2)}) copy-start(bf16[32,2048,64]{1,2,0:T(8,128)(2,1)} %gather_fusion.2) | copy-start | bytes 25165828
  284.5 4.7 %copy-start.3 = (bf16[1,64,1024]{2,1,0:T(8,128)(2,1)S(1)}, bf16[1,64,1024]{2,1,0:T(8,128)(2,1)}, u32[]{:S(2)}) copy-start(bf16[1,64,1024]{2,1,0:T(8,128)(2,1)} %param.7) | copy-start | bytes 393220
  290.4 18.5 %copy-start.1 = (bf16[64,1024]{1,0:T(8,128)(2,1)}, bf16[64,1024]{1,0:T(8,128)(2,1)S(1)}, u32[]{:S(2)}) copy-start(bf16[64,1024]{1,0:T(8,128)(2,1)S(1)} %get-tuple-element.5) | copy-start | bytes 393220
Sparse Core Ops, SparseCore 0:
  14.2 111.4 all-gather.6
  127.2 105.9 all-gather.8
Sparse Core Ops, SparseCore 1:
  33.3 28.6 reduce-scatter.2
  64.3 25.7 reduce-scatter.4
where the time goes:
time: 317 us; the launch traced here: 316 us
  waiting for transfers between devices  141 us (44%)
  blocking collectives  61.8 us (19%)
  local copies, waits for them, and re-layouts  58.7 us (19%)
  matrix products  36.9 us (12%)
  between operations  15.6 us (5%)
    all_gather x2, waiting for transfers between devices, shards(): lax.all_gather(layer_down_factor, ('req', 'pair'), axis=0, tiled=True)  140 us
    gather x2, local copies, waits for them, and re-layouts, shards(): blocks = whole_pool[ids_own]  22.3 us
    dot_general x2, matrix products, shards(): lax.dot_general(weight_layer, context_all, (((0,), (1,)), ((), ())), pref...  19.6 us
    psum x1, blocking collectives, shards(): shrink_own = lax.psum(partial_value, 'tensor').astype(jnp.bfloat16)  19 us
    gather x2, local copies, waits for them, and re-layouts, shards(): selected_up_factor = adapter_up_factors[layer_number][index_half_split]  17.9 us
    psum x1, blocking collectives, shards(): squares = lax.psum(jnp.sum(wide * wide, axis=-1), ('tensor', 'req'))  17.7 us
    all_gather x2, blocking collectives, shards(): context_all = lax.all_gather(context_own, 'req', axis=0, tiled=True)  16.2 us
    squeeze x1, local copies, waits for them, and re-layouts, shards(): selected_up_factor = adapter_up_factors[layer_number][index_half_split]  12.3 us
  transfers between devices with their start and end apart: 4, of which 2 were waited for; matrix products, arithmetic and copies ran while one was open for 28% of the time, Pallas kernels for 0%

commit v1 on v0

--- a/solution.py
+++ b/solution.py
@@ -1,6 +1,10 @@
+import functools
+
 import jax
 import jax.numpy as jnp
 from jax import lax
+from jax.experimental import pallas as pl
+from jax.experimental.pallas import tpu as pltpu
 from jax.sharding import PartitionSpec as P
 
 MODEL_WIDTH = 8192
@@ -11,7 +15,7 @@
 norm_eps = 1e-05
 
 
-def shards(
+def plain_shards(
     residual_input,
     contexts,
     projection_weight,
@@ -69,7 +73,337 @@
     return (hidden_state[None], normed.astype(jnp.bfloat16)[None])
 
 
+def offsets(sizes):
+    t_size, r_size, p_size = sizes
+    return [
+        (dt, dr, dp)
+        for dt in range(t_size)
+        for dr in range(r_size)
+        for dp in range(p_size)
+        if (dt, dr, dp) != (0, 0, 0)
+    ]
+
+
+def fused_kernel(
+    sizes,
+    res_ref, ctx_ref, w_ref, d_ref, u_ref, gain_ref, ids_ref,
+    out_ref, norm_ref,
+    wbuf, dbuf, ubuf, cbuf, part, rs_buf, shr, own_sum, zsend, zrecv, delta, swap, sq_buf, sq_recv,
+    w_sem, d_sem, u_sem, c_send, c_recv, rs_send, rs_recv, ag_send, ag_recv,
+    z_send, z_recv, p_send, p_recv, n_send, n_recv,
+):
+    t_size, r_size, p_size = sizes
+    t = lax.axis_index("tensor")
+    r = lax.axis_index("req")
+    p = lax.axis_index("pair")
+    layers, _, rows_own, k_size = ctx_ref.shape
+    half = rows_own * r_size
+    rows = half * p_size
+    cols = res_ref.shape[2]
+    ncol = cols // p_size
+    pool = u_ref.shape[1]
+    rank = 64
+
+    def dev(dt, dr, dp):
+        return {
+            "tensor": lax.rem(t + dt, t_size),
+            "req": lax.rem(r + dr, r_size),
+            "pair": lax.rem(p + dp, p_size),
+        }
+
+    def number(d):
+        return (d["tensor"] * r_size + d["req"]) * p_size + d["pair"]
+
+    def remote(src, dst, ssem, rsem, target):
+        return pltpu.make_async_remote_copy(
+            src_ref=src, dst_ref=dst, send_sem=ssem, recv_sem=rsem,
+            device_id=target, device_id_type=pl.DeviceIdType.MESH,
+        )
+
+    if t_size == 4:
+        blocks = [3 - t, lax.rem(t + 2, 4), t + 1 - 2 * lax.rem(t, 2), t]
+    else:
+        blocks = [lax.rem(t + j + 1, t_size) for j in range(t_size)]
+
+    d_copies = [
+        pltpu.make_async_copy(d_ref.at[l], dbuf.at[l], d_sem.at[l]) for l in range(layers)
+    ]
+    w_copies = [
+        [
+            pltpu.make_async_copy(
+                w_ref.at[l, :, pl.ds(pl.multiple_of(blocks[j] * cols + p * ncol, ncol), ncol)],
+                wbuf.at[j, l],
+                w_sem.at[j, l],
+            )
+            for l in range(layers)
+        ]
+        for j in range(t_size)
+    ]
+    u_copies = [
+        pltpu.make_async_copy(
+            u_ref.at[l, :, pl.ds(pl.multiple_of(p * ncol, ncol), ncol)], ubuf.at[l], u_sem.at[l]
+        )
+        for l in range(layers)
+    ]
+    for c in d_copies:
+        c.start()
+    for js in w_copies:
+        for c in js:
+            c.start()
+    for c in u_copies:
+        c.start()
+
+    barrier = pltpu.get_barrier_semaphore()
+    offs = offsets(sizes)
+    for o in offs:
+        pl.semaphore_signal(
+            barrier, inc=1, device_id=dev(*o), device_id_type=pl.DeviceIdType.MESH
+        )
+    pl.semaphore_wait(barrier, len(offs))
+
+    row_own = pl.multiple_of(p * half + r * rows_own, rows_own)
+    row_far = pl.multiple_of(p * half + (1 - r) * rows_own, rows_own)
+    x_copies, m_copies, f_copies = [], [], []
+    for l in range(layers):
+        x_copies.append(remote(
+            ctx_ref.at[l, 0], cbuf.at[l, pl.ds(row_own, rows_own)],
+            c_send.at[0, l], c_recv.at[0, l], dev(0, 1, 0)))
+        m_copies.append(remote(
+            ctx_ref.at[l, 0], cbuf.at[l, pl.ds(row_own, rows_own)],
+            c_send.at[1, l], c_recv.at[1, l], dev(0, 0, 1)))
+        f_copies.append(remote(
+            cbuf.at[l, pl.ds(row_far, rows_own)], cbuf.at[l, pl.ds(row_far, rows_own)],
+            c_send.at[2, l], c_recv.at[2, l], dev(0, 0, 1)))
+    for c in x_copies:
+        c.start()
+    for c in m_copies:
+        c.start()
+    for l in range(layers):
+        cbuf[l, pl.ds(row_own, rows_own), :] = ctx_ref[l, 0]
+
+    lane = lax.broadcasted_iota(jnp.int32, (rows, 128), 1)
+    low = lane < rank
+    upper = jnp.where(low, 0, 1)
+    id_rows = ids_ref[...].astype(jnp.float32)
+    id_row = jnp.concatenate([id_rows[h : h + 1] for h in range(p_size)], axis=1)
+    id_mat = jnp.broadcast_to(id_row, (rows, rows)).T.astype(jnp.int32)
+
+    for l in range(layers):
+        x_copies[l].wait_recv()
+        f_copies[l].start()
+    for l in range(layers):
+        m_copies[l].wait_recv()
+        f_copies[l].wait_recv()
+
+    own_base = (r * p_size + p) * (dbuf.shape[1] // rank)
+    folded = []
+    for l in range(layers):
+        d_copies[l].wait()
+        wide = lax.dot_general(
+            cbuf[l], dbuf[l], (((1,), (1,)), ((), ())), preferred_element_type=jnp.float32
+        )
+        total = jnp.zeros((rows, 128), jnp.float32)
+        for k in range(dbuf.shape[1] // 128):
+            use = id_mat == own_base + 2 * k + upper
+            total = total + jnp.where(use, wide[:, k * 128 : (k + 1) * 128], 0.0)
+        folded.append(total + pltpu.roll(total, rank, 1))
+    part[...] = jnp.where(low, folded[0], folded[1])
+
+    me = {"tensor": t, "req": r, "pair": p}
+    mine = number(me)
+    piece = part.shape[0] // (len(offs) + 1)
+    rs_copies = []
+    for i, o in enumerate(offs):
+        target = dev(*o)
+        c = remote(
+            part.at[pl.ds(pl.multiple_of(number(target) * piece, piece), piece)],
+            rs_buf.at[i], rs_send.at[i], rs_recv.at[i], target)
+        c.start()
+        rs_copies.append(c)
+
+    def project(j):
+        acc = None
+        for l in range(layers):
+            w_copies[j][l].wait()
+            term = jnp.dot(cbuf[l], wbuf[j, l], preferred_element_type=jnp.float32)
+            acc = term if acc is None else acc + term
+        return acc
+
+    z_copies = []
+
+    def project_and_send(j):
+        zsend[j] = project(j).astype(jnp.bfloat16)
+        target = {"tensor": blocks[j], "req": r, "pair": p}
+        c = remote(zsend.at[j], zrecv.at[j], z_send.at[j], z_recv.at[j], target)
+        c.start()
+        z_copies.append(c)
+
+    project_and_send(0)
+
+    for c in rs_copies:
+        c.wait_recv()
+    at_mine = pl.ds(pl.multiple_of(mine * piece, piece), piece)
+    total = part[at_mine, :]
+    for i in range(len(offs)):
+        total = total + rs_buf[i]
+    shr[at_mine, :] = total.astype(jnp.bfloat16).astype(jnp.float32)
+    ag_copies = []
+    for i, o in enumerate(offs):
+        c = remote(shr.at[at_mine], shr.at[at_mine], ag_send.at[i], ag_recv.at[i], dev(*o))
+        c.start()
+        ag_copies.append(c)
+
+    for j in range(1, t_size - 1):
+        project_and_send(j)
+    own_sum[...] = project(t_size - 1)
+
+    for i in range(len(offs)):
+        ag_copies[i].wait_recv()
+    shrink = shr[...]
+    other = pltpu.roll(shrink, rank, 1)
+    expand = None
+    for l in range(layers):
+        u_copies[l].wait()
+        both = jnp.where(low, shrink, other) if l == 0 else jnp.where(low, other, shrink)
+        placed = jnp.concatenate(
+            [
+                jnp.where(id_mat == 2 * k + upper, both, 0.0).astype(jnp.bfloat16)
+                for k in range(pool // 128)
+            ],
+            axis=1,
+        )
+        term = jnp.dot(placed, ubuf[l], preferred_element_type=jnp.float32)
+        expand = term if expand is None else expand + term
+    own_sum[...] += adapter_scale * expand
+
+    for c in z_copies:
+        c.wait_recv()
+    acc = own_sum[...]
+    for j in range(t_size - 1):
+        acc = acc + zrecv[j].astype(jnp.float32)
+    delta[...] = acc
+
+    give = pl.ds(pl.multiple_of((1 - p) * half, half), half)
+    keep = pl.ds(pl.multiple_of(p * half, half), half)
+    swap_copy = remote(
+        delta.at[give], swap, p_send.at[0], p_recv.at[0], dev(0, 0, 1))
+    swap_copy.start()
+    swap_copy.wait_recv()
+    kept, got = delta[keep, :], swap[...]
+    first = p == 0
+    left = jnp.where(first, kept, got)
+    right = jnp.where(first, got, kept)
+    hidden = []
+    for q, add in enumerate((left, right)):
+        at = slice(q * ncol, (q + 1) * ncol)
+        value = (res_ref[0, :, at].astype(jnp.float32) + add).astype(jnp.bfloat16)
+        out_ref[0, :, at] = value
+        hidden.append(value.astype(jnp.float32))
+    sq = jnp.zeros((half, 128), jnp.float32)
+    for value in hidden:
+        for k in range(ncol // 128):
+            tile = value[:, k * 128 : (k + 1) * 128]
+            sq = sq + tile * tile
+    padded = jnp.concatenate([sq, jnp.zeros((128 - half, 128), jnp.float32)], axis=0) if half < 128 else sq
+    sq_row = jnp.sum(padded.T, axis=0, keepdims=True)
+    sq_buf[...] = jnp.broadcast_to(sq_row, sq_buf.shape)
+    n_copies = []
+    n_offs = [o for o in offs if o[2] == 0]
+    for i, o in enumerate(n_offs):
+        c = remote(sq_buf, sq_recv.at[i], n_send.at[i], n_recv.at[i], dev(*o))
+        c.start()
+        n_copies.append(c)
+    for c in n_copies:
+        c.wait_recv()
+    sums = sq_buf[...]
+    for i in range(len(n_offs)):
+        sums = sums + sq_recv[i]
+    inverse = lax.rsqrt(sums[0:1] / MODEL_WIDTH + norm_eps)
+    scale = jnp.broadcast_to(inverse, (128, 128)).T[:half]
+    for q, value in enumerate(hidden):
+        for k in range(ncol // 128):
+            at = q * ncol + k * 128
+            g = gain_ref[at // 128 : at // 128 + 1, :].astype(jnp.float32)
+            tile = value[:, k * 128 : (k + 1) * 128]
+            norm_ref[0, :, at : at + 128] = (tile * scale * g).astype(jnp.bfloat16)
+
+    for group in (x_copies, m_copies, f_copies, rs_copies, ag_copies, z_copies, [swap_copy], n_copies):
+        for c in group:
+            c.wait_send()
+
+
+def fits(sizes, residual_input, contexts, adapter_down_factors, adapter_up_factors):
+    t_size, r_size, p_size = sizes
+    layers, _, rows_own, k_size = contexts.shape
+    rows = rows_own * r_size * p_size
+    rank = adapter_down_factors.shape[3]
+    return (
+        t_size == 4 and r_size == 2 and p_size == 2 and layers == 2 and rows == 128
+        and rank == 64 and rows_own % 16 == 0 and residual_input.shape[2] % 256 == 0
+        and adapter_up_factors.shape[1] % 2 == 0 and adapter_down_factors.shape[1] % 2 == 0
+        and k_size % 128 == 0
+    )
+
+
+def shards(sizes, *args):
+    (residual_input, contexts, projection_weight, adapter_down_factors, adapter_up_factors,
+     norm_gain_vector, request_adapter_index) = args
+    if not fits(sizes, residual_input, contexts, adapter_down_factors, adapter_up_factors):
+        return plain_shards(*args)
+    t_size, r_size, p_size = sizes
+    layers, _, rows_own, k_size = contexts.shape
+    half = rows_own * r_size
+    rows = half * p_size
+    cols = residual_input.shape[2]
+    ncol = cols // p_size
+    own, rank = adapter_down_factors.shape[1], adapter_down_factors.shape[3]
+    down = jnp.swapaxes(adapter_down_factors, 2, 3).reshape(layers, own * rank, k_size)
+    pool = adapter_up_factors.shape[1] * rank
+    up = adapter_up_factors.reshape(layers, pool, cols)
+    gain = norm_gain_vector.reshape(cols // 128, 128)
+    peers = t_size * r_size * p_size - 1
+    n_peers = t_size * r_size - 1
+    piece = rows // (peers + 1)
+    vmem = pl.BlockSpec(memory_space=pltpu.VMEM)
+    hbm = pl.BlockSpec(memory_space=pl.ANY)
+    dma = pltpu.SemaphoreType.DMA
+    return pl.pallas_call(
+        functools.partial(fused_kernel, sizes),
+        out_shape=(
+            jax.ShapeDtypeStruct(residual_input.shape, jnp.bfloat16),
+            jax.ShapeDtypeStruct(residual_input.shape, jnp.bfloat16),
+        ),
+        in_specs=[vmem, vmem, hbm, hbm, hbm, vmem, vmem],
+        out_specs=(vmem, vmem),
+        scratch_shapes=[
+            pltpu.VMEM((t_size, layers, k_size, ncol), jnp.bfloat16),
+            pltpu.VMEM((layers, own * rank, k_size), jnp.bfloat16),
+            pltpu.VMEM((layers, pool, ncol), jnp.bfloat16),
+            pltpu.VMEM((layers, rows, k_size), jnp.bfloat16),
+            pltpu.VMEM((rows, 128), jnp.float32),
+            pltpu.VMEM((peers, piece, 128), jnp.float32),
+            pltpu.VMEM((rows, 128), jnp.float32),
+            pltpu.VMEM((rows, ncol), jnp.float32),
+            pltpu.VMEM((t_size - 1, rows, ncol), jnp.bfloat16),
+            pltpu.VMEM((t_size - 1, rows, ncol), jnp.bfloat16),
+            pltpu.VMEM((rows, ncol), jnp.float32),
+            pltpu.VMEM((half, ncol), jnp.float32),
+            pltpu.VMEM((8, 128), jnp.float32),
+            pltpu.VMEM((n_peers, 8, 128), jnp.float32),
+            dma((t_size, layers)), dma((layers,)), dma((layers,)),
+            dma((3, layers)), dma((3, layers)),
+            dma((peers,)), dma((peers,)), dma((peers,)), dma((peers,)),
+            dma((t_size - 1,)), dma((t_size - 1,)),
+            dma((1,)), dma((1,)), dma((n_peers,)), dma((n_peers,)),
+        ],
+        compiler_params=pltpu.CompilerParams(
+            collective_id=0, has_side_effects=True, vmem_limit_bytes=48 * 1024 * 1024
+        ),
+    )(residual_input, contexts, projection_weight, down, up, gain, request_adapter_index)
+
+
 def solution(mesh):
+    sizes = (mesh.shape["tensor"], mesh.shape["req"], mesh.shape["pair"])
     in_specs = (
         P(("groups", "pair"), None, ("req", "tensor")),
         P(None, ("groups", "pair"), "req", "tensor"),
@@ -83,4 +417,4 @@
         P(("groups", "pair"), None, ("req", "tensor")),
         P(("groups", "pair"), None, ("req", "tensor")),
     )
-    return jax.shard_map(shards, mesh=mesh, in_specs=in_specs, out_specs=out_specs, check_vma=False)
+    return jax.shard_map(functools.partial(shards, sizes), mesh=mesh, in_specs=in_specs, out_specs=out_specs, check_vma=False)

time: 317 us -> 45.6 us (0.14)
  waiting for transfers between devices: 141 us -> 0 us
  blocking collectives: 61.8 us -> 0 us
  local copies, waits for them, and re-layouts: 58.7 us -> 4.52 us
  Pallas kernels: 0 us -> 40.3 us
  matrix products: 36.9 us -> 0 us
  between operations: 15.6 us -> 0.65 us
    all_gather x2 -> x0, waiting for transfers between devices: 140 us -> none  [shards(): lax.all_gather(layer_down_factor, ('req', 'pair'), axis=0, tiled=True)]
    gather x4 -> x0, local copies, waits for them, and re-layouts: 40.3 us -> none  [the longest x2 22.3 us: shards(): blocks = whole_pool[ids_own]]
    pallas_call x0 -> x1, Pallas kernels: none -> 40.3 us  [shards(): pl.pallas_call(functools.partial(fused_kernel, sizes), out_shape=(jax.Sha...]
    dot_general x6 -> x0, matrix products: 36.9 us -> none  [the longest x2 19.6 us: shards(): lax.dot_general(weight_layer, context_all, (((0,), (1,)), ((), ())), pref...]
    psum x2 -> x0, blocking collectives: 36.7 us -> none  [the longest x1 19 us: shards(): shrink_own = lax.psum(partial_value, 'tensor').astype(jnp.bfloat16)]
    all_gather x4 -> x0, blocking collectives: 25.1 us -> none  [the longest x2 16.2 us: shards(): context_all = lax.all_gather(context_own, 'req', axis=0, tiled=True)]
    squeeze x1 -> x0, local copies, waits for them, and re-layouts: 12.3 us -> none  [shards(): selected_up_factor = adapter_up_factors[layer_number][index_half_split]]
  transfers between devices with their start and end apart: 4 -> 0, of which waited for: 2 -> 0; matrix products, arithmetic and copies ran while one was open for 28% -> 0% of each run, Pallas kernels for 0% -> 0%
where the time goes in v1:
time: 45.6 us; the launch traced here: 45.4 us
  Pallas kernels  40.3 us (88%)
  local copies, waits for them, and re-layouts  4.52 us (10%)
  between operations  0.65 us (1%)
    pallas_call x1, Pallas kernels, shards(): pl.pallas_call(functools.partial(fused_kernel, sizes), out_shape=(jax.Sha...  40.3 us
    unnamed x10, local copies, waits for them, and re-layouts  4.52 us

profile of v1, /device:TPU:0, one launch (start us, length us, event | category | flops | bytes accessed | tf_op | source)
XLA Modules:
  0.0 45.4 jit_solution(12298206879045872409)
XLA Ops:
  0.6 0.0 copy-start
  0.6 0.9 %copy-done = bf16[2,1,32,2048]{3,2,1,0:T(8,128)(2,1)S(1)} copy-done((bf16[2,1,32,2048]{3,2,1,0:T(8,128)(2,1)S(1)}, bf16[2,1,32,2048]{3,2,1,0:T(8,128)(2,1)}, u32[]{:S(2)}) %copy-start) | copy-done | bytes 262168
  1.6 0.0 copy-start.1
  1.6 0.9 %copy-done.1 = bf16[1,64,1024]{2,1,0:T(8,128)(2,1)S(1)} copy-done((bf16[1,64,1024]{2,1,0:T(8,128)(2,1)S(1)}, bf16[1,64,1024]{2,1,0:T(8,128)(2,1)}, u32[]{:S(2)}) %copy-start.1) | copy-done | bytes 131096
  2.5 0.0 copy-start.2
  2.5 0.7 %copy-done.2 = bf16[1024]{0:T(1024)(128)(2,1)S(1)} copy-done((bf16[1024]{0:T(1024)(128)(2,1)S(1)}, bf16[1024]{0:T(1024)(128)(2,1)}, u32[]{:S(2)}) %copy-start.2) | copy-done | bytes 2072
  3.2 0.0 copy-start.3
  3.2 0.7 %copy-done.3 = s32[2,64]{1,0:T(2,128)S(1)} copy-done((s32[2,64]{1,0:T(2,128)S(1)}, s32[2,64]{1,0:T(2,128)}, u32[]{:S(2)}) %copy-start.3) | copy-done | bytes 536
  3.8 40.3 %shard_map.86 = (bf16[1,64,1024]{2,1,0:T(8,128)(2,1)S(1)}, bf16[1,64,1024]{2,1,0:T(8,128)(2,1)S(1)}) custom-call(bf16[1,64,1024]{2,1,0:T(8,128)(2,1)S(1)} %copy-done.1, bf16[2,1,32,2048]{3,2,1,0:T(8,128)(2,1)S(1)} %copy-done, bf16[2,2048,4096]{2,1,0:T(8,128)(2,1)} %w_ref.1, bf16[2,1024,2048]{2,1,0:T(8,128)(2,1)} %bitcast.7, bf16[2,4096,1024]{2,1,0:T(8,128)(2,1)} %bitcast.6, ...), custom_call_target="tpu_custom_call" | custom-call | tf_op jit(solution)/shard_map/pallas_call | solution.py:370
  44.1 0.7 %copy.11 = bf16[1,64,1024]{2,1,0:T(8,128)(2,1)} copy(bf16[1,64,1024]{2,1,0:T(8,128)(2,1)S(1)} %get-tuple-element.4) | data formatting | bytes 262144
  44.8 0.7 %copy.12 = bf16[1,64,1024]{2,1,0:T(8,128)(2,1)} copy(bf16[1,64,1024]{2,1,0:T(8,128)(2,1)S(1)} %get-tuple-element.5) | data formatting | bytes 262144
Async XLA Ops:
  0.6 1.0 %copy-start = (bf16[2,1,32,2048]{3,2,1,0:T(8,128)(2,1)S(1)}, bf16[2,1,32,2048]{3,2,1,0:T(8,128)(2,1)}, u32[]{:S(2)}) copy-start(bf16[2,1,32,2048]{3,2,1,0:T(8,128)(2,1)} %ctx_ref.1) | copy-start | bytes 786436
  1.6 0.9 %copy-start.1 = (bf16[1,64,1024]{2,1,0:T(8,128)(2,1)S(1)}, bf16[1,64,1024]{2,1,0:T(8,128)(2,1)}, u32[]{:S(2)}) copy-start(bf16[1,64,1024]{2,1,0:T(8,128)(2,1)} %res_ref.1) | copy-start | bytes 393220
  2.5 0.7 %copy-start.2 = (bf16[1024]{0:T(1024)(128)(2,1)S(1)}, bf16[1024]{0:T(1024)(128)(2,1)}, u32[]{:S(2)}) copy-start(bf16[1024]{0:T(1024)(128)(2,1)} %param.12) | copy-start | bytes 6148
  3.2 0.7 %copy-start.3 = (s32[2,64]{1,0:T(2,128)S(1)}, s32[2,64]{1,0:T(2,128)}, u32[]{:S(2)}) copy-start(s32[2,64]{1,0:T(2,128)} %ids_ref.1) | copy-start | bytes 1540

commit v2 on v1

--- a/solution.py
+++ b/solution.py
@@ -88,8 +88,9 @@
     sizes,
     res_ref, ctx_ref, w_ref, d_ref, u_ref, gain_ref, ids_ref,
     out_ref, norm_ref,
+    res_buf, gain_buf, id_buf, id_buf_wide,
     wbuf, dbuf, ubuf, cbuf, part, rs_buf, shr, own_sum, zsend, zrecv, delta, swap, sq_buf, sq_recv,
-    w_sem, d_sem, u_sem, c_send, c_recv, rs_send, rs_recv, ag_send, ag_recv,
+    in_sem, w_sem, d_sem, u_sem, c_send, c_recv, rs_send, rs_recv, ag_send, ag_recv,
     z_send, z_recv, p_send, p_recv, n_send, n_recv,
 ):
     t_size, r_size, p_size = sizes
@@ -99,7 +100,7 @@
     layers, _, rows_own, k_size = ctx_ref.shape
     half = rows_own * r_size
     rows = half * p_size
-    cols = res_ref.shape[2]
+    cols = res_buf.shape[2]
     ncol = cols // p_size
     pool = u_ref.shape[1]
     rank = 64
@@ -145,12 +146,23 @@
         )
         for l in range(layers)
     ]
-    for c in d_copies:
-        c.start()
-    for js in w_copies:
+    row_own = pl.multiple_of(r * 2 * rows_own + p * rows_own, rows_own)
+    row_far = pl.multiple_of((1 - r) * 2 * rows_own + p * rows_own, rows_own)
+    own_copies = [
+        pltpu.make_async_copy(ctx_ref.at[l, 0], cbuf.at[l, pl.ds(row_own, rows_own)], in_sem.at[l])
+        for l in range(layers)
+    ]
+    small_copies = [
+        pltpu.make_async_copy(ids_ref, id_buf, in_sem.at[layers]),
+        pltpu.make_async_copy(res_ref, res_buf, in_sem.at[layers + 1]),
+        pltpu.make_async_copy(gain_ref, gain_buf, in_sem.at[layers + 2]),
+    ]
+    for c in own_copies + small_copies[:1]:
+        c.start()
+    for js in w_copies[:-1]:
         for c in js:
             c.start()
-    for c in u_copies:
+    for c in d_copies + w_copies[-1] + u_copies + small_copies[1:]:
         c.start()
 
     barrier = pltpu.get_barrier_semaphore()
@@ -161,8 +173,6 @@
         )
     pl.semaphore_wait(barrier, len(offs))
 
-    row_own = pl.multiple_of(p * half + r * rows_own, rows_own)
-    row_far = pl.multiple_of(p * half + (1 - r) * rows_own, rows_own)
     x_copies, m_copies, f_copies = [], [], []
     for l in range(layers):
         x_copies.append(remote(
@@ -174,40 +184,109 @@
         f_copies.append(remote(
             cbuf.at[l, pl.ds(row_far, rows_own)], cbuf.at[l, pl.ds(row_far, rows_own)],
             c_send.at[2, l], c_recv.at[2, l], dev(0, 0, 1)))
+    for c in m_copies:
+        c.start()
     for c in x_copies:
         c.start()
-    for c in m_copies:
-        c.start()
-    for l in range(layers):
-        cbuf[l, pl.ds(row_own, rows_own), :] = ctx_ref[l, 0]
 
     lane = lax.broadcasted_iota(jnp.int32, (rows, 128), 1)
     low = lane < rank
     upper = jnp.where(low, 0, 1)
-    id_rows = ids_ref[...].astype(jnp.float32)
-    id_row = jnp.concatenate([id_rows[h : h + 1] for h in range(p_size)], axis=1)
+    small_copies[0].wait()
+    id_rows = id_buf[...].astype(jnp.float32)
+    id_row = jnp.concatenate(
+        [
+            id_rows[h : h + 1, q * rows_own : (q + 1) * rows_own]
+            for q in range(r_size)
+            for h in range(p_size)
+        ],
+        axis=1,
+    )
     id_mat = jnp.broadcast_to(id_row, (rows, rows)).T.astype(jnp.int32)
 
+    near = pl.ds(pl.multiple_of(r * half, half), half)
+    far = pl.ds(pl.multiple_of((1 - r) * half, half), half)
+
+    def project(j, at, first):
+        acc = None
+        for l in range(layers):
+            if first:
+                w_copies[j][l].wait()
+            term = jnp.dot(cbuf[l, at, :], wbuf[j, l], preferred_element_type=jnp.float32)
+            acc = term if acc is None else acc + term
+        return acc
+
+    z_copies = []
+
+    outer = lax.rem(t // 2 + lax.rem(t, 2) + 1, 2)
+    near_t = t + 1 - 2 * lax.rem(t, 2)
+    relay = t_size - 1
+
+    def z_copy(j, at, side):
+        slot, target = j, blocks[j]
+        if j == 0:
+            slot = outer * relay
+            target = outer * near_t + (1 - outer) * blocks[0]
+        return remote(
+            zsend.at[j, at], zrecv.at[slot, at], z_send.at[side, j], z_recv.at[side, slot],
+            {"tensor": target, "req": r, "pair": p})
+
+    def arrived(j, at, side):
+        return remote(
+            zsend.at[0, at], zrecv.at[j, at], z_send.at[side, 0], z_recv.at[side, j],
+            {"tensor": near_t, "req": r, "pair": p})
+
+    def project_and_send(j, at, side):
+        value = project(j, at, side == 0)
+        if j == 1:
+            own_sum[at, :] = value
+
+            @pl.when(outer == 0)
+            def _():
+                arrived(relay, at, side).wait_recv()
+                own_sum[at, :] += zrecv[relay, at, :].astype(jnp.float32)
+
+            value = own_sum[at, :]
+        zsend[j, at, :] = value.astype(jnp.bfloat16)
+        c = z_copy(j, at, side)
+        c.start()
+        z_copies.append(c)
+
+    own_base = (r * p_size + p) * (dbuf.shape[1] // rank)
+    id_buf_wide[...] = id_mat
+
+    def shrink_rows(at):
+        low_half = low[:half]
+        ids_at = id_buf_wide[at, :]
+        folded = []
+        for l in range(layers):
+            wide = lax.dot_general(
+                cbuf[l, at, :], dbuf[l], (((1,), (1,)), ((), ())),
+                preferred_element_type=jnp.float32,
+            )
+            total = jnp.zeros((half, 128), jnp.float32)
+            for k in range(dbuf.shape[1] // 128):
+                use = ids_at == own_base + 2 * k + upper[:half]
+                total = total + jnp.where(use, wide[:, k * 128 : (k + 1) * 128], 0.0)
+            folded.append(total + pltpu.roll(total, rank, 1))
+        part[at, :] = jnp.where(low_half, folded[0], folded[1])
+
     for l in range(layers):
-        x_copies[l].wait_recv()
-        f_copies[l].start()
+        own_copies[l].wait()
+        m_copies[l].wait_recv()
+    for j in (0, 2, 1):
+        project_and_send(j, near, 0)
+        if j == 0:
+            x_copies[0].wait_recv()
+            f_copies[0].start()
+    x_copies[1].wait_recv()
+    f_copies[1].start()
+    for c in d_copies:
+        c.wait()
+    shrink_rows(near)
     for l in range(layers):
-        m_copies[l].wait_recv()
         f_copies[l].wait_recv()
-
-    own_base = (r * p_size + p) * (dbuf.shape[1] // rank)
-    folded = []
-    for l in range(layers):
-        d_copies[l].wait()
-        wide = lax.dot_general(
-            cbuf[l], dbuf[l], (((1,), (1,)), ((), ())), preferred_element_type=jnp.float32
-        )
-        total = jnp.zeros((rows, 128), jnp.float32)
-        for k in range(dbuf.shape[1] // 128):
-            use = id_mat == own_base + 2 * k + upper
-            total = total + jnp.where(use, wide[:, k * 128 : (k + 1) * 128], 0.0)
-        folded.append(total + pltpu.roll(total, rank, 1))
-    part[...] = jnp.where(low, folded[0], folded[1])
+    shrink_rows(far)
 
     me = {"tensor": t, "req": r, "pair": p}
     mine = number(me)
@@ -221,24 +300,7 @@
         c.start()
         rs_copies.append(c)
 
-    def project(j):
-        acc = None
-        for l in range(layers):
-            w_copies[j][l].wait()
-            term = jnp.dot(cbuf[l], wbuf[j, l], preferred_element_type=jnp.float32)
-            acc = term if acc is None else acc + term
-        return acc
-
-    z_copies = []
-
-    def project_and_send(j):
-        zsend[j] = project(j).astype(jnp.bfloat16)
-        target = {"tensor": blocks[j], "req": r, "pair": p}
-        c = remote(zsend.at[j], zrecv.at[j], z_send.at[j], z_recv.at[j], target)
-        c.start()
-        z_copies.append(c)
-
-    project_and_send(0)
+    project_and_send(0, far, 1)
 
     for c in rs_copies:
         c.wait_recv()
@@ -253,9 +315,9 @@
         c.start()
         ag_copies.append(c)
 
-    for j in range(1, t_size - 1):
-        project_and_send(j)
-    own_sum[...] = project(t_size - 1)
+    for j in (2, 1):
+        project_and_send(j, far, 1)
+    own_sum[...] = project(t_size - 1, slice(None), True)
 
     for i in range(len(offs)):
         ag_copies[i].wait_recv()
@@ -276,27 +338,47 @@
         expand = term if expand is None else expand + term
     own_sum[...] += adapter_scale * expand
 
-    for c in z_copies:
-        c.wait_recv()
+    for side, at in enumerate((near, far)):
+        for j in (1, 2):
+            arrived(j, at, side).wait_recv()
+
+        @pl.when(outer == 0)
+        def _():
+            arrived(0, at, side).wait_recv()
+            own_sum[at, :] += zrecv[0, at, :].astype(jnp.float32)
+
     acc = own_sum[...]
-    for j in range(t_size - 1):
+    for j in (1, 2):
         acc = acc + zrecv[j].astype(jnp.float32)
     delta[...] = acc
 
-    give = pl.ds(pl.multiple_of((1 - p) * half, half), half)
-    keep = pl.ds(pl.multiple_of(p * half, half), half)
-    swap_copy = remote(
-        delta.at[give], swap, p_send.at[0], p_recv.at[0], dev(0, 0, 1))
-    swap_copy.start()
-    swap_copy.wait_recv()
-    kept, got = delta[keep, :], swap[...]
+    swap_copies = []
+    for q in range(r_size):
+        give = pl.ds(pl.multiple_of(q * half + (1 - p) * rows_own, rows_own), rows_own)
+        c = remote(
+            delta.at[give], swap.at[pl.ds(q * rows_own, rows_own)],
+            p_send.at[q], p_recv.at[q], dev(0, 0, 1))
+        c.start()
+        swap_copies.append(c)
+    kept = jnp.concatenate(
+        [
+            delta[pl.ds(pl.multiple_of(q * half + p * rows_own, rows_own), rows_own), :]
+            for q in range(r_size)
+        ],
+        axis=0,
+    )
+    for c in small_copies[1:]:
+        c.wait()
+    for c in swap_copies:
+        c.wait_recv()
+    got = swap[...]
     first = p == 0
     left = jnp.where(first, kept, got)
     right = jnp.where(first, got, kept)
     hidden = []
     for q, add in enumerate((left, right)):
         at = slice(q * ncol, (q + 1) * ncol)
-        value = (res_ref[0, :, at].astype(jnp.float32) + add).astype(jnp.bfloat16)
+        value = (res_buf[0, :, at].astype(jnp.float32) + add).astype(jnp.bfloat16)
         out_ref[0, :, at] = value
         hidden.append(value.astype(jnp.float32))
     sq = jnp.zeros((half, 128), jnp.float32)
@@ -323,11 +405,11 @@
     for q, value in enumerate(hidden):
         for k in range(ncol // 128):
             at = q * ncol + k * 128
-            g = gain_ref[at // 128 : at // 128 + 1, :].astype(jnp.float32)
+            g = gain_buf[at // 128 : at // 128 + 1, :].astype(jnp.float32)
             tile = value[:, k * 128 : (k + 1) * 128]
             norm_ref[0, :, at : at + 128] = (tile * scale * g).astype(jnp.bfloat16)
 
-    for group in (x_copies, m_copies, f_copies, rs_copies, ag_copies, z_copies, [swap_copy], n_copies):
+    for group in (x_copies, m_copies, f_copies, rs_copies, ag_copies, z_copies, swap_copies, n_copies):
         for c in group:
             c.wait_send()
 
@@ -365,7 +447,7 @@
     n_peers = t_size * r_size - 1
     piece = rows // (peers + 1)
     vmem = pl.BlockSpec(memory_space=pltpu.VMEM)
-    hbm = pl.BlockSpec(memory_space=pl.ANY)
+    hbm = pl.BlockSpec(memory_space=pltpu.HBM)
     dma = pltpu.SemaphoreType.DMA
     return pl.pallas_call(
         functools.partial(fused_kernel, sizes),
@@ -373,9 +455,13 @@
             jax.ShapeDtypeStruct(residual_input.shape, jnp.bfloat16),
             jax.ShapeDtypeStruct(residual_input.shape, jnp.bfloat16),
         ),
-        in_specs=[vmem, vmem, hbm, hbm, hbm, vmem, vmem],
+        in_specs=[hbm] * 7,
         out_specs=(vmem, vmem),
         scratch_shapes=[
+            pltpu.VMEM(residual_input.shape, jnp.bfloat16),
+            pltpu.VMEM(gain.shape, jnp.bfloat16),
+            pltpu.VMEM(request_adapter_index.shape, jnp.int32),
+            pltpu.VMEM((rows, 128), jnp.int32),
             pltpu.VMEM((t_size, layers, k_size, ncol), jnp.bfloat16),
             pltpu.VMEM((layers, own * rank, k_size), jnp.bfloat16),
             pltpu.VMEM((layers, pool, ncol), jnp.bfloat16),
@@ -385,19 +471,19 @@
             pltpu.VMEM((rows, 128), jnp.float32),
             pltpu.VMEM((rows, ncol), jnp.float32),
             pltpu.VMEM((t_size - 1, rows, ncol), jnp.bfloat16),
-            pltpu.VMEM((t_size - 1, rows, ncol), jnp.bfloat16),
+            pltpu.VMEM((t_size, rows, ncol), jnp.bfloat16),
             pltpu.VMEM((rows, ncol), jnp.float32),
             pltpu.VMEM((half, ncol), jnp.float32),
             pltpu.VMEM((8, 128), jnp.float32),
             pltpu.VMEM((n_peers, 8, 128), jnp.float32),
-            dma((t_size, layers)), dma((layers,)), dma((layers,)),
+            dma((layers + 3,)), dma((t_size, layers)), dma((layers,)), dma((layers,)),
             dma((3, layers)), dma((3, layers)),
             dma((peers,)), dma((peers,)), dma((peers,)), dma((peers,)),
-            dma((t_size - 1,)), dma((t_size - 1,)),
-            dma((1,)), dma((1,)), dma((n_peers,)), dma((n_peers,)),
+            dma((2, t_size - 1)), dma((2, t_size)),
+            dma((r_size,)), dma((r_size,)), dma((n_peers,)), dma((n_peers,)),
         ],
         compiler_params=pltpu.CompilerParams(
-            collective_id=0, has_side_effects=True, vmem_limit_bytes=48 * 1024 * 1024
+            collective_id=0, has_side_effects=True, vmem_limit_bytes=62 * 1024 * 1024
         ),
     )(residual_input, contexts, projection_weight, down, up, gain, request_adapter_index)
 

time: 45.6 us -> 40.5 us (0.89)
  Pallas kernels: 40.3 us -> 36.6 us
  local copies, waits for them, and re-layouts: 4.52 us -> 3.14 us
    pallas_call x1, Pallas kernels: 40.3 us -> 36.6 us  [shards(): pl.pallas_call(functools.partial(fused_kernel, sizes), out_shape=(jax.Sha...]
    unnamed x10 -> x2, local copies, waits for them, and re-layouts: 4.52 us -> 3.14 us
where the time goes in v2:
time: 40.5 us; the launch traced here: 40.4 us
  Pallas kernels  36.6 us (90%)
  local copies, waits for them, and re-layouts  3.14 us (8%)
  between operations  0.64 us (2%)
    pallas_call x1, Pallas kernels, shards(): pl.pallas_call(functools.partial(fused_kernel, sizes), out_shape=(jax.Sha...  36.6 us
    unnamed x2, local copies, waits for them, and re-layouts  3.14 us

profile of v2, /device:TPU:0, one launch (start us, length us, event | category | flops | bytes accessed | tf_op | source)
XLA Modules:
  0.0 40.4 jit_solution(71691627093284214)
XLA Ops:
  0.6 36.6 %shard_map.86 = (bf16[1,64,1024]{2,1,0:T(8,128)(2,1)}, bf16[1,64,1024]{2,1,0:T(8,128)(2,1)}) custom-call(bf16[1,64,1024]{2,1,0:T(8,128)(2,1)} %res_ref.1, bf16[2,1,32,2048]{3,2,1,0:T(8,128)(2,1)} %ctx_ref.1, bf16[2,2048,4096]{2,1,0:T(8,128)(2,1)} %w_ref.1, bf16[2,1024,2048]{2,1,0:T(8,128)(2,1)} %bitcast.6, bf16[2,4096,1024]{2,1,0:T(8,128)(2,1)} %bitcast.5, ...), custom_call_target="tpu_custom_call" | custom-call | tf_op jit(solution)/shard_map/pallas_call | solution.py:452
  37.2 1.6 %copy.11 = bf16[1,64,1024]{2,1,0:T(8,128)(2,1)} copy(bf16[1,64,1024]{2,1,0:T(8,128)(2,1)} %get-tuple-element.4) | data formatting | bytes 262144
  38.8 1.6 %copy.12 = bf16[1,64,1024]{2,1,0:T(8,128)(2,1)} copy(bf16[1,64,1024]{2,1,0:T(8,128)(2,1)} %get-tuple-element.5) | data formatting | bytes 262144
